TPU v7x, 32 devices: a whole 2x2x4 slice. The times are simulated.
32 devices in a mesh: orb: 8 (over z, core), bas: 4 (over y, x).
Axes of the slice: x: 2, y: 2, z: 4, core: 2. Of those that a mesh axis runs over, the one named last changes fastest.
Arguments:
- coeffs: bfloat16 [131072, 1024], P('bas', 'orb'), may hold values from -6 to 6
- dipole: bfloat16 [3, 4, 32768, 384], P(None, 'bas', 'orb'), may hold values from -0.0008544922 to 0.0008544922
- tile_cols: int32 [4, 256, 3], P('bas', 'orb'), may hold values from -1 to 31, as said below
- matching: int32 [1, 8], replicated, may hold values from 0 to 7, as said below
Outputs:
- localized: bfloat16 [131072, 1024], P('bas', 'orb')
Inputs may be any that keep to these rules, and one draw needn't show every extreme that they name: `tile_cols`: entry [b, r, s] is the column tile of slot s of row tile r of basis block b, counted within the row tile's group of 32 tiles, or -1 for a padded slot; slot 0 is the row tile itself, and the live slots of a row name distinct tiles. `matching`: each row pairs every block with another block and is its own inverse; the rows are distinct rounds of one round-robin tournament.
All inputs are finite; a program needn't handle non-finite values.
Results may differ from a plain program's by a relative error of at most 0.0047.
Values may be sent and summed in bfloat16 or wider, within the bound.
A program may use at most 192 MiB of HBM per device.

v0:
```python
import jax
import jax.numpy as jnp
from jax import lax
from jax.sharding import PartitionSpec as P

BLK = 128
TILE = 128
SLOTS = 3
SWEEPS = 4


def jacobi_pair(gram):
    highest = lax.Precision.HIGHEST
    half = gram.shape[1] // 2
    positions = jnp.arange(half, dtype=jnp.int32)
    accum = jnp.eye(2 * half, dtype=jnp.float32)
    for sweep_index in range(SWEEPS):
        permute = jnp.equal(positions[None, :], (positions[:, None] + sweep_index) % half).astype(
            jnp.float32
        )
        diag_vals = jnp.diagonal(gram, axis1=1, axis2=2)
        head_vals = diag_vals[:, :half]
        tail_vals = jnp.roll(diag_vals[:, half:], -sweep_index, axis=1)
        off_vals = jnp.diagonal(
            jnp.roll(gram[:, :half, half:], -sweep_index, axis=2), axis1=1, axis2=2
        )
        spread = head_vals - tail_vals
        quad_term = jnp.sum(off_vals * off_vals - 0.25 * spread * spread, axis=0)
        lin_term = jnp.sum(off_vals * spread, axis=0)
        angles = 0.25 * jnp.arctan(lin_term / (jnp.abs(quad_term) + 1.0))
        cosine = jnp.cos(angles)
        sine_part = jnp.sin(angles)
        upper_half = jnp.concatenate([jnp.diag(cosine), -(sine_part[:, None] * permute)], axis=1)
        bottom = jnp.concatenate(
            [permute.T * sine_part[None, :], jnp.diag(jnp.roll(cosine, sweep_index))], axis=1
        )
        rotation = jnp.concatenate([upper_half, bottom], axis=0)
        gram = jnp.einsum(
            "ji,kjl->kil",
            rotation,
            jnp.einsum("kij,jl->kil", gram, rotation, precision=highest),
            precision=highest,
        )
        accum = jnp.dot(accum, rotation, precision=highest)
    return accum


def project_rows(dipole_rows, tile_index, local_rows, blocks):
    group_tiles = tile_index.shape[0]
    tile_rows = local_rows.reshape(group_tiles, TILE, blocks * BLK)
    picked = tile_rows[jnp.maximum(tile_index, 0)]
    picked = jnp.where((tile_index >= 0)[:, :, None, None], picked, jnp.zeros_like(picked))
    picked = picked.reshape(group_tiles, SLOTS * TILE, blocks * BLK)
    moments = jnp.einsum(
        "kraj,rjn->kran", dipole_rows, picked, preferred_element_type=jnp.float32
    ).astype(jnp.bfloat16)
    return moments.reshape(3, group_tiles * TILE, blocks, BLK)


def gram_terms(coef_blocks, moment_blocks, partner, leader, follower):
    raw_gram = jnp.einsum(
        "rbi,krbj->bkij", coef_blocks, moment_blocks, preferred_element_type=jnp.float32
    )
    self_gram = 0.5 * (raw_gram + jnp.swapaxes(raw_gram, 2, 3))
    toward = jnp.einsum(
        "rbi,krbj->bkij",
        coef_blocks,
        moment_blocks[:, :, partner],
        preferred_element_type=jnp.float32,
    )
    cross_gram = 0.5 * (toward[leader] + jnp.swapaxes(toward[follower], 2, 3))
    return (self_gram, cross_gram)


def body(coeffs, dipole, tile_cols, matching):
    local_rows = lax.all_to_all(coeffs, "orb", split_axis=0, concat_axis=1, tiled=True)
    blocks = lax.axis_size("orb")
    my_block = lax.axis_index("orb")
    row_count = local_rows.shape[0]
    dipole_rows = dipole[:, 0].reshape(3, tile_cols.shape[1], TILE, SLOTS * TILE)
    tile_index = tile_cols[0]
    block_ids = jnp.arange(blocks, dtype=jnp.int32)
    partner = matching[0]
    leader = jnp.minimum(block_ids, partner)
    follower = jnp.maximum(block_ids, partner)
    moments = project_rows(dipole_rows, tile_index, local_rows, blocks)
    coef_blocks = local_rows.reshape(row_count, blocks, BLK)
    self_gram, cross_gram = gram_terms(coef_blocks, moments, partner, leader, follower)
    my_leader = leader[my_block]
    entries = jnp.stack([self_gram[leader], self_gram[follower], cross_gram], axis=1)
    summed = lax.psum_scatter(entries, "orb", scatter_dimension=0, tiled=True)[0]
    summed = lax.psum(summed, "bas")
    lead_gram = summed[0]
    follow_gram = summed[1]
    cross_mine = summed[2]
    upper_half = jnp.concatenate([lead_gram, cross_mine], axis=2)
    lower_half = jnp.concatenate([jnp.swapaxes(cross_mine, 1, 2), follow_gram], axis=2)
    rotor = jacobi_pair(jnp.concatenate([upper_half, lower_half], axis=1))
    weight = jnp.where(my_leader == my_block, rotor[:, :BLK], rotor[:, BLK:]).astype(jnp.bfloat16)
    weights = lax.all_gather(weight[None], "orb", axis=0, tiled=True)
    is_lead = (leader == block_ids)[:, None, None]
    self_weight = jnp.where(is_lead, weights[:, :BLK], weights[:, BLK:])
    other_weight = jnp.where(is_lead, weights[:, BLK:], weights[:, :BLK])
    rotated = jnp.einsum(
        "rbj,bjn->rbn", coef_blocks, self_weight, preferred_element_type=jnp.float32
    )
    rotated = rotated + jnp.einsum(
        "rbj,bjn->rbn", coef_blocks[:, partner], other_weight, preferred_element_type=jnp.float32
    )
    local_rows = rotated.astype(jnp.bfloat16).reshape(row_count, blocks * BLK)
    return lax.all_to_all(local_rows, "orb", split_axis=1, concat_axis=0, tiled=True)


def solution(mesh):
    in_specs = (P("bas", "orb"), P(None, "bas", "orb", None), P("bas", "orb", None), P())
    out_specs = P("bas", "orb")
    return jax.shard_map(body, mesh=mesh, in_specs=in_specs, out_specs=out_specs, check_vma=False)
```

profile of v0, /device:TPU:0, one launch (start us, length us, event | category | flops | bytes accessed | tf_op | source)
XLA Modules:
  0.0 982.3 jit_solution(16487530379932482928)
XLA Ops:
  6.5 6.5 all-to-all-start
  14.1 182.9 %all-to-all-done = bf16[8,4096,128]{2,1,0:T(8,128)(2,1)} async-done(((bf16[8,4096,128]{2,1,0:T(8,128)(2,1)}), bf16[8,4096,128]{2,1,0:T(8,128)(2,1)}, u32[]{:S(2)}, u32[]{:S(2)}) %all-to-all-start) | async-done | bytes 8388640 | tf_op jit(solution)/shard_map/all_to_all | solution.py:76
  197.0 10.3 %copy.135 = bf16[4096,8,128]{2,1,0:T(8,128)(2,1)} copy(bf16[4096,8,128]{2,0,1:T(8,128)(2,1)} %bitcast.4) | data formatting | bytes 16777216 | tf_op jit(solution)/shard_map/all_to_all | solution.py:76
  207.3 13.3 %reshape.298 = bf16[32,128,1024]{2,1,0:T(8,128)(2,1)} reshape(bf16[4096,8,128]{2,1,0:T(8,128)(2,1)} %copy.135) | data formatting | bytes 16777216 | tf_op jit(solution)/shard_map/reshape | solution.py:50
  220.6 13.6 %gather_fusion = bf16[96,128,1024]{2,1,0:T(8,128)(2,1)} fusion(bf16[32,128,1024]{2,1,0:T(8,128)(2,1)} %reshape.298, s32[1024]{0:T(1024)S(1)} %pad_clamp_fusion.3), kind=kCustom, calls=%fused_computation | custom fusion | bytes 50332032 | tf_op jit(solution)/shard_map/gather | solution.py:51
  234.2 20.9 %bitcast_select_fusion = bf16[32,384,1024]{2,1,0:T(8,128)(2,1)} fusion(pred[32,384]{1,0:T(8,128)(4,1)S(1)} %bitcast.185, bf16[32,384,1024]{2,1,0:T(8,128)(2,1)} %bitcast.176), kind=kLoop, calls=%fused_computation.22 | loop fusion | flops 12582912 | bytes 50343936 | tf_op jit(solution)/shard_map/jit(_where)/select_n | solution.py:52
  255.1 25.8 %convert_bitcast_fusion = bf16[3,32,128,1024]{2,3,0,1:T(8,128)(2,1)} fusion(bf16[32,384,1024]{2,1,0:T(8,128)(2,1)} %bitcast_select_fusion, bf16[3,32,128,384]{3,2,1,0:T(8,128)(2,1)} %bitcast.200), kind=kOutput, calls=%fused_computation.23 | convolution fusion | flops 9676259328 | bytes 59768832 | tf_op jit(solution)/shard_map/kraj,rjn->kran/dot_general | solution.py:54
  281.0 32.6 %copy.139 = bf16[3,32,128,1024]{3,2,1,0:T(8,128)(2,1)} copy(bf16[3,32,128,1024]{2,3,0,1:T(8,128)(2,1)} %convert_bitcast_fusion) | data formatting | bytes 50331648 | tf_op jit(solution)/shard_map/convert_element_type | solution.py:56
  313.5 23.2 %copy.185 = bf16[1536,8,8,128]{3,2,1,0:T(8,128)(2,1)} copy(bf16[1536,8,8,128]{3,1,2,0:T(8,128)(2,1)} %bitcast.174) | data formatting | bytes 50331648
  336.7 31.7 %copy.140 = bf16[3,4096,8,128]{1,3,0,2:T(8,128)(2,1)} copy(bf16[3,4096,8,128]{3,2,1,0:T(8,128)(2,1)} %bitcast.175) | data formatting | bytes 50331648 | tf_op jit(solution)/shard_map/reshape | solution.py:57
  368.4 17.8 %fusion.95 = (bf16[3,2048,8,128]{1,3,0,2:T(8,128)(2,1)}, bf16[3,2048,8,128]{1,3,0,2:T(8,128)(2,1)}) fusion(bf16[3,4096,8,128]{1,3,0,2:T(8,128)(2,1)} %copy.140), kind=kLoop, calls=%fused_computation.191 | loop fusion | bytes 50331648 | tf_op jit(solution)/shard_map/gather | solution.py:68
  386.2 10.9 %gather_fusion.14 = bf16[8,3,2048,128]{2,3,1,0:T(8,128)(2,1)} fusion(bf16[3,2048,8,128]{1,3,0,2:T(8,128)(2,1)} %get-tuple-element.21, s32[1024]{0:T(1024)S(1)} %get-tuple-element.40), kind=kCustom, calls=%fused_computation.14 | custom fusion | bytes 25165856 | tf_op jit(solution)/shard_map/gather | solution.py:68
  397.1 10.9 %gather_fusion.15 = bf16[8,3,2048,128]{2,3,1,0:T(8,128)(2,1)} fusion(bf16[3,2048,8,128]{1,3,0,2:T(8,128)(2,1)} %get-tuple-element.22, s32[1024]{0:T(1024)S(1)} %get-tuple-element.40), kind=kCustom, calls=%fused_computation.15 | custom fusion | bytes 25165856 | tf_op jit(solution)/shard_map/gather | solution.py:68
  408.0 14.5 %fusion.19 = f32[8,3,128,128]{2,3,1,0:T(8,128)S(1)} fusion(bf16[8,4096,128]{2,1,0:T(8,128)(2,1)} %all-to-all-done, bf16[3,2048,8,128]{1,3,0,2:T(8,128)(2,1)} %bitcast.179, bf16[3,2048,8,128]{1,3,0,2:T(8,128)(2,1)} %bitcast.178), kind=kOutput, calls=%fused_computation.37 | convolution fusion | flops 3271557120 | bytes 35127296 | tf_op jit(solution)/shard_map/rbi,krbj->bkij/dot_general | solution.py:65
  422.5 1.6 copy.144
  424.1 1.9 gather_fusion.4
  426.0 14.0 %fusion.11 = f32[8,3,128,128]{3,2,1,0:T(8,128)S(1)} fusion(bf16[3,4096,8,128]{1,3,0,2:T(8,128)(2,1)} %copy.140, bf16[8,4096,128]{2,1,0:T(8,128)(2,1)} %all-to-all-done), kind=kOutput, calls=%fused_computation.28 | convolution fusion | flops 3221225472 | bytes 35127296 | tf_op jit(solution)/shard_map/rbi,krbj->bkij/dot_general | solution.py:61
  440.0 1.6 copy.141
  441.6 1.6 fusion.18
  443.8 1.9 gather_fusion.1
  445.8 3.4 gather_fusion.3
  449.2 2.1 fusion.17
  451.4 2.6 pad_maximum_fusion
  454.7 104.7 %all-reduce.6.cloned.1.call-done = f32[8,3,3,128,128]{4,3,2,0,1:T(8,128)} async-done(((f32[8,3,3,128,128]{4,3,2,0,1:T(8,128)}), f32[8,3,3,128,128]{4,3,2,0,1:T(8,128)}) %all-reduce.6.cloned.1.call-update) | async-done | bytes 4718608
  559.4 2.6 dynamic-slice_bitcast_fusion
  563.4 8.2 gather_fusion.13
  571.6 37.0 %all-reduce.4.cloned.1.call-done = f32[3,3,128,128]{3,2,1,0:T(8,128)} async-done(((f32[3,3,128,128]{3,2,1,0:T(8,128)}), f32[3,3,128,128]{3,2,1,0:T(8,128)}) %all-reduce.4.cloned.1.call-update) | async-done | bytes 589840 | tf_op jit(solution)/shard_map/psum | solution.py:92
  609.9 4.6 copy.145
  614.5 1.9 gather_fusion.5
  616.6 16.9 %copy.148 = f32[3,256,256]{0,2,1:T(8,128)} copy(f32[3,256,256]{2,1,0:T(8,128)S(1)} %maximum_maximum_fusion) | data formatting | bytes 1572864 | tf_op jit(solution)/shard_map/concatenate | solution.py:98
  633.4 2.3 gather_fusion.6
  638.2 16.7 %copy.153 = f32[3,256,256]{0,2,1:T(8,128)} copy(f32[3,256,256]{1,2,0:T(8,128)S(1)} %convolution_bitcast_fusion.2) | data formatting | bytes 1572864 | tf_op jit(solution)/shard_map/ji,kjl->kil/transpose | solution.py:38
  654.9 2.3 gather_fusion.8
  657.4 7.5 copy.151
  664.9 1.9 gather_fusion.7
  670.4 16.9 %copy.159 = f32[3,256,256]{0,2,1:T(8,128)} copy(f32[3,256,256]{1,2,0:T(8,128)S(1)} %convolution_bitcast_fusion.1) | data formatting | bytes 1572864 | tf_op jit(solution)/shard_map/ji,kjl->kil/transpose | solution.py:38
  687.4 2.3 gather_fusion.10
  689.9 7.5 copy.157
  697.4 1.9 gather_fusion.9
  701.8 16.7 %copy.165 = f32[3,256,256]{0,2,1:T(8,128)} copy(f32[3,256,256]{1,2,0:T(8,128)S(1)} %convolution_bitcast_fusion) | data formatting | bytes 1572864 | tf_op jit(solution)/shard_map/ji,kjl->kil/transpose | solution.py:38
  718.5 2.3 gather_fusion.12
  721.0 7.5 copy.163
  728.5 1.9 gather_fusion.11
  732.3 15.0 %all-gather = bf16[2048,128]{1,0:T(8,128)(2,1)S(1)} all-gather(bf16[256,128]{1,0:T(8,128)(2,1)S(1)} %fusion.47), channel_id=2, replica_groups=mesh['orb'=8,'bas'=4] {'orb'}, dimensions={0}, use_global_device_ids=true | all-gather | bytes 589824 | tf_op jit(solution)/shard_map/all_gather | solution.py:100
  747.7 11.5 %fusion.42 = f32[8,128,4096]{2,1,0:T(8,128)} fusion(bf16[8,128,128]{1,2,0:T(8,128)(2,1)S(1)} %copy.182, bf16[8,128,128]{1,2,0:T(8,128)(2,1)S(1)} %copy.183, pred[8]{0:T(512)(128)(4,1)S(1)} %iota_compare_fusion.11, bf16[8,4096,128]{2,1,0:T(8,128)(2,1)} %all-to-all-done), kind=kOutput, calls=%fused_computation.64 | convolution fusion | flops 1073872896 | bytes 25690120 | tf_op jit(solution)/shard_map/rbj,bjn->rbn/dot_general | solution.py:104
  759.2 14.0 %fusion.13 = bf16[4096,8,128]{0,2,1:T(8,128)(2,1)} fusion(f32[8,128,4096]{2,1,0:T(8,128)} %fusion.42, bf16[8,4096,128]{2,1,0:T(8,128)(2,1)} %gather_fusion.13, bf16[8,128,128]{1,2,0:T(8,128)(2,1)S(1)} %copy.183, bf16[8,128,128]{1,2,0:T(8,128)(2,1)S(1)} %copy.182, pred[8]{0:T(512)(128)(4,1)S(1)} %iota_compare_fusion.11), kind=kOutput, calls=%fused_computation.30 | convolution fusion | flops 1082261504 | bytes 34078728 | tf_op jit(solution)/shard_map/rbj,bjn->rbn/dot_general | solution.py:107
  773.3 189.9 %all_to_all.32 = bf16[4096,8,128]{0,2,1:T(8,128)(2,1)} all-to-all(bf16[4096,8,128]{0,2,1:T(8,128)(2,1)} %fusion.13), channel_id=1, replica_groups=mesh['orb'=8,'bas'=4] {'orb'}, dimensions={1} | all-to-all | bytes 16777216 | tf_op jit(solution)/shard_map/all_to_all | solution.py:111
  963.1 11.9 %copy.169 = bf16[8,4096,128]{2,1,0:T(8,128)(2,1)} copy(bf16[8,4096,128]{1,2,0:T(8,128)(2,1)} %bitcast.177) | data formatting | bytes 16777216 | tf_op jit(solution)/shard_map/all_to_all | solution.py:111
  (105 shorter events, 15.7 us)
Async XLA Ops:
  6.5 6.5 copy-start.1
  6.5 7.0 copy-start.2
  6.5 190.5 %all-to-all-start = ((bf16[8,4096,128]{2,1,0:T(8,128)(2,1)}), bf16[8,4096,128]{2,1,0:T(8,128)(2,1)}, u32[]{:S(2)}, u32[]{:S(2)}) async-start(bf16[8,4096,128]{2,1,0:T(8,128)(2,1)} %bitcast.180), calls=%async_computation | async-start | bytes 16777216 | tf_op jit(solution)/shard_map/all_to_all | solution.py:76
  13.0 546.4 %all-reduce.6.cloned.1.call-start = ((), (), s32[]{:S(2)}) async-start(), calls=%async_computation.3 | async-start | bytes 9437184
  445.8 5.6 copy-start
  449.2 4.8 copy-start.4
  449.2 5.5 copy-start.3
  454.0 154.6 %all-reduce.4.cloned.1.call-start = ((), (), s32[]{:S(2)}) async-start(), calls=%async_computation.2 | async-start | bytes 1179648 | tf_op jit(solution)/shard_map/psum | solution.py:92
Sparse Core Ops, SparseCore 0:
  454.1 105.2 all-reduce.5
  562.4 46.1 all-reduce.3
where the time goes:
time: 994 us; the launch traced here: 982 us
  waiting for transfers between devices  325 us (33%)
  local copies, waits for them, and re-layouts  314 us (32%)
  blocking collectives  205 us (21%)
  matrix products  86.3 us (9%)
  other arithmetic  30.6 us (3%)
  between operations  15.1 us (2%)
    all_to_all x1, blocking collectives, body(): lax.all_to_all(local_rows, 'orb', split_axis=1, concat_axis=0, tiled=True)  190 us
    all_to_all x1, waiting for transfers between devices, body(): lax.all_to_all(coeffs, 'orb', split_axis=0, concat_axis=1, tiled=True)  183 us
    unnamed x3, waiting for transfers between devices  105 us
    transpose x3, local copies, waits for them, and re-layouts, jacobi_pair(): jnp.einsum('ji,kjl->kil', rotation, jnp.einsum('kij,jl->kil', gram, rotat...  50.4 us
    gather x3, local copies, waits for them, and re-layouts, gram_terms(): moment_blocks[:, :, partner]  39.6 us
    psum x1, waiting for transfers between devices, body(): summed = lax.psum(summed, 'bas')  37 us
    convert_element_type x1, local copies, waits for them, and re-layouts, project_rows(): moments = jnp.einsum('kraj,rjn->kran', dipole_rows, picked, preferred_ele...  32.6 us
    reshape x1, local copies, waits for them, and re-layouts, project_rows(): return moments.reshape(3, group_tiles * TILE, blocks, BLK)  31.7 us
  transfers between devices with their start and end apart: 3, of which 3 were waited for; matrix products, arithmetic and copies ran while one was open for 1% of the time, Pallas kernels for 0%

commit v1 on v0

--- a/solution.py
+++ b/solution.py
@@ -89,7 +89,8 @@
     my_leader = leader[my_block]
     entries = jnp.stack([self_gram[leader], self_gram[follower], cross_gram], axis=1)
     summed = lax.psum_scatter(entries, "orb", scatter_dimension=0, tiled=True)[0]
-    summed = lax.psum(summed, "bas")
+    shards = lax.all_gather(summed, "bas", axis=0, tiled=False)
+    summed = shards.sum(axis=0)
     lead_gram = summed[0]
     follow_gram = summed[1]
     cross_mine = summed[2]

time: 994 us -> 986 us (level)
    psum x1 -> x0, waiting for transfers between devices: 37 us -> none  [body(): summed = lax.psum(summed, 'bas')]
    all_gather x0 -> x1, waiting for transfers between devices: none -> 28 us  [body(): shards = lax.all_gather(summed, 'bas', axis=0, tiled=False)]
    unnamed x15 -> x16, local copies, waits for them, and re-layouts: 24.2 us -> 26.8 us
where the time goes in v1:
time: 986 us; the launch traced here: 974 us
  waiting for transfers between devices  316 us (32%)
  local copies, waits for them, and re-layouts  313 us (32%)
  blocking collectives  205 us (21%)
  matrix products  86.3 us (9%)
  other arithmetic  32.4 us (3%)
  between operations  15.1 us (2%)
    all_to_all x1, blocking collectives, body(): lax.all_to_all(local_rows, 'orb', split_axis=1, concat_axis=0, tiled=True)  190 us
    all_to_all x1, waiting for transfers between devices, body(): lax.all_to_all(coeffs, 'orb', split_axis=0, concat_axis=1, tiled=True)  183 us
    unnamed x3, waiting for transfers between devices  105 us
    transpose x3, local copies, waits for them, and re-layouts, jacobi_pair(): jnp.einsum('ji,kjl->kil', rotation, jnp.einsum('kij,jl->kil', gram, rotat...  50.4 us
    gather x3, local copies, waits for them, and re-layouts, gram_terms(): moment_blocks[:, :, partner]  39.6 us
    convert_element_type x1, local copies, waits for them, and re-layouts, project_rows(): moments = jnp.einsum('kraj,rjn->kran', dipole_rows, picked, preferred_ele...  32.6 us
    reshape x1, local copies, waits for them, and re-layouts, project_rows(): return moments.reshape(3, group_tiles * TILE, blocks, BLK)  31.7 us
    all_gather x1, waiting for transfers between devices, body(): shards = lax.all_gather(summed, 'bas', axis=0, tiled=False)  28 us
  transfers between devices with their start and end apart: 3, of which 3 were waited for; matrix products, arithmetic and copies ran while one was open for 1% of the time, Pallas kernels for 0%

profile of v1, /device:TPU:0, one launch (start us, length us, event | category | flops | bytes accessed | tf_op | source)
XLA Modules:
  0.0 974.2 jit_solution(9588552163212918512)
XLA Ops:
  6.5 6.5 all-to-all-start
  14.1 182.9 %all-to-all-done = bf16[8,4096,128]{2,1,0:T(8,128)(2,1)} async-done(((bf16[8,4096,128]{2,1,0:T(8,128)(2,1)}), bf16[8,4096,128]{2,1,0:T(8,128)(2,1)}, u32[]{:S(2)}, u32[]{:S(2)}) %all-to-all-start) | async-done | bytes 8388640 | tf_op jit(solution)/shard_map/all_to_all | solution.py:76
  197.0 10.3 %copy.135 = bf16[4096,8,128]{2,1,0:T(8,128)(2,1)} copy(bf16[4096,8,128]{2,0,1:T(8,128)(2,1)} %bitcast.4) | data formatting | bytes 16777216 | tf_op jit(solution)/shard_map/all_to_all | solution.py:76
  207.3 13.3 %reshape.298 = bf16[32,128,1024]{2,1,0:T(8,128)(2,1)} reshape(bf16[4096,8,128]{2,1,0:T(8,128)(2,1)} %copy.135) | data formatting | bytes 16777216 | tf_op jit(solution)/shard_map/reshape | solution.py:50
  220.6 13.6 %gather_fusion = bf16[96,128,1024]{2,1,0:T(8,128)(2,1)} fusion(bf16[32,128,1024]{2,1,0:T(8,128)(2,1)} %reshape.298, s32[1024]{0:T(1024)S(1)} %pad_clamp_fusion.3), kind=kCustom, calls=%fused_computation | custom fusion | bytes 50332032 | tf_op jit(solution)/shard_map/gather | solution.py:51
  234.2 20.9 %bitcast_select_fusion = bf16[32,384,1024]{2,1,0:T(8,128)(2,1)} fusion(pred[32,384]{1,0:T(8,128)(4,1)S(1)} %bitcast.183, bf16[32,384,1024]{2,1,0:T(8,128)(2,1)} %bitcast.174), kind=kLoop, calls=%fused_computation.22 | loop fusion | flops 12582912 | bytes 50343936 | tf_op jit(solution)/shard_map/jit(_where)/select_n | solution.py:52
  255.1 25.8 %convert_bitcast_fusion = bf16[3,32,128,1024]{2,3,0,1:T(8,128)(2,1)} fusion(bf16[32,384,1024]{2,1,0:T(8,128)(2,1)} %bitcast_select_fusion, bf16[3,32,128,384]{3,2,1,0:T(8,128)(2,1)} %bitcast.198), kind=kOutput, calls=%fused_computation.23 | convolution fusion | flops 9676259328 | bytes 59768832 | tf_op jit(solution)/shard_map/kraj,rjn->kran/dot_general | solution.py:54
  281.0 32.6 %copy.139 = bf16[3,32,128,1024]{3,2,1,0:T(8,128)(2,1)} copy(bf16[3,32,128,1024]{2,3,0,1:T(8,128)(2,1)} %convert_bitcast_fusion) | data formatting | bytes 50331648 | tf_op jit(solution)/shard_map/convert_element_type | solution.py:56
  313.5 23.2 %copy.185 = bf16[1536,8,8,128]{3,2,1,0:T(8,128)(2,1)} copy(bf16[1536,8,8,128]{3,1,2,0:T(8,128)(2,1)} %bitcast.172) | data formatting | bytes 50331648
  336.7 31.7 %copy.140 = bf16[3,4096,8,128]{1,3,0,2:T(8,128)(2,1)} copy(bf16[3,4096,8,128]{3,2,1,0:T(8,128)(2,1)} %bitcast.173) | data formatting | bytes 50331648 | tf_op jit(solution)/shard_map/reshape | solution.py:57
  368.4 17.8 %fusion.95 = (bf16[3,2048,8,128]{1,3,0,2:T(8,128)(2,1)}, bf16[3,2048,8,128]{1,3,0,2:T(8,128)(2,1)}) fusion(bf16[3,4096,8,128]{1,3,0,2:T(8,128)(2,1)} %copy.140), kind=kLoop, calls=%fused_computation.191 | loop fusion | bytes 50331648 | tf_op jit(solution)/shard_map/gather | solution.py:68
  386.2 10.9 %gather_fusion.14 = bf16[8,3,2048,128]{2,3,1,0:T(8,128)(2,1)} fusion(bf16[3,2048,8,128]{1,3,0,2:T(8,128)(2,1)} %get-tuple-element.21, s32[1024]{0:T(1024)S(1)} %get-tuple-element.40), kind=kCustom, calls=%fused_computation.14 | custom fusion | bytes 25165856 | tf_op jit(solution)/shard_map/gather | solution.py:68
  397.1 10.9 %gather_fusion.15 = bf16[8,3,2048,128]{2,3,1,0:T(8,128)(2,1)} fusion(bf16[3,2048,8,128]{1,3,0,2:T(8,128)(2,1)} %get-tuple-element.22, s32[1024]{0:T(1024)S(1)} %get-tuple-element.40), kind=kCustom, calls=%fused_computation.15 | custom fusion | bytes 25165856 | tf_op jit(solution)/shard_map/gather | solution.py:68
  408.0 14.5 %fusion.19 = f32[8,3,128,128]{2,3,1,0:T(8,128)S(1)} fusion(bf16[8,4096,128]{2,1,0:T(8,128)(2,1)} %all-to-all-done, bf16[3,2048,8,128]{1,3,0,2:T(8,128)(2,1)} %bitcast.177, bf16[3,2048,8,128]{1,3,0,2:T(8,128)(2,1)} %bitcast.176), kind=kOutput, calls=%fused_computation.37 | convolution fusion | flops 3271557120 | bytes 35127296 | tf_op jit(solution)/shard_map/rbi,krbj->bkij/dot_general | solution.py:65
  422.5 1.6 copy.144
  424.1 1.9 gather_fusion.4
  426.0 14.0 %fusion.11 = f32[8,3,128,128]{3,2,1,0:T(8,128)S(1)} fusion(bf16[3,4096,8,128]{1,3,0,2:T(8,128)(2,1)} %copy.140, bf16[8,4096,128]{2,1,0:T(8,128)(2,1)} %all-to-all-done), kind=kOutput, calls=%fused_computation.28 | convolution fusion | flops 3221225472 | bytes 35127296 | tf_op jit(solution)/shard_map/rbi,krbj->bkij/dot_general | solution.py:61
  440.0 1.6 copy.141
  443.8 1.9 gather_fusion.1
  445.8 3.4 gather_fusion.3
  449.2 2.1 fusion.17
  451.4 2.6 pad_maximum_fusion
  454.7 104.7 %all-reduce.3.cloned.1.call-done = f32[8,3,3,128,128]{4,3,2,0,1:T(8,128)} async-done(((f32[8,3,3,128,128]{4,3,2,0,1:T(8,128)}), f32[8,3,3,128,128]{4,3,2,0,1:T(8,128)}) %all-reduce.3.cloned.1.call-update) | async-done | bytes 4718608
  559.4 2.6 constant_dynamic-slice_fusion
  563.4 8.3 gather_fusion.13
  571.7 28.0 %all-gather.3.cloned.1.call-done = f32[4,3,3,128,128]{4,3,2,0,1:T(8,128)} async-done(((f32[1,3,3,128,128]{4,3,2,0,1:T(8,128)}), f32[4,3,3,128,128]{4,3,2,0,1:T(8,128)}) %all-gather.3.cloned.1.call-update) | async-done | bytes 2359312 | tf_op jit(solution)/shard_map/all_gather | solution.py:92
  599.7 1.9 reduce_sum.81
  601.8 4.6 copy.145
  606.4 1.9 gather_fusion.5
  608.4 16.9 %copy.148 = f32[3,256,256]{0,2,1:T(8,128)} copy(f32[3,256,256]{2,1,0:T(8,128)S(1)} %maximum_maximum_fusion) | data formatting | bytes 1572864 | tf_op jit(solution)/shard_map/concatenate | solution.py:99
  625.3 2.3 gather_fusion.6
  630.1 16.7 %copy.153 = f32[3,256,256]{0,2,1:T(8,128)} copy(f32[3,256,256]{1,2,0:T(8,128)S(1)} %convolution_bitcast_fusion.2) | data formatting | bytes 1572864 | tf_op jit(solution)/shard_map/ji,kjl->kil/transpose | solution.py:38
  646.8 2.3 gather_fusion.8
  649.3 7.5 copy.151
  656.8 1.9 gather_fusion.7
  662.3 16.9 %copy.159 = f32[3,256,256]{0,2,1:T(8,128)} copy(f32[3,256,256]{1,2,0:T(8,128)S(1)} %convolution_bitcast_fusion.1) | data formatting | bytes 1572864 | tf_op jit(solution)/shard_map/ji,kjl->kil/transpose | solution.py:38
  679.3 2.3 gather_fusion.10
  681.8 7.5 copy.157
  689.3 1.9 gather_fusion.9
  693.6 16.7 %copy.165 = f32[3,256,256]{0,2,1:T(8,128)} copy(f32[3,256,256]{1,2,0:T(8,128)S(1)} %convolution_bitcast_fusion) | data formatting | bytes 1572864 | tf_op jit(solution)/shard_map/ji,kjl->kil/transpose | solution.py:38
  710.4 2.3 gather_fusion.12
  712.9 7.5 copy.163
  720.4 1.9 gather_fusion.11
  724.2 15.0 %all-gather = bf16[2048,128]{1,0:T(8,128)(2,1)S(1)} all-gather(bf16[256,128]{1,0:T(8,128)(2,1)S(1)} %fusion.47), channel_id=2, replica_groups=mesh['orb'=8,'bas'=4] {'orb'}, dimensions={0}, use_global_device_ids=true | all-gather | bytes 589824 | tf_op jit(solution)/shard_map/all_gather | solution.py:101
  739.6 11.5 %fusion.42 = f32[8,128,4096]{2,1,0:T(8,128)} fusion(bf16[8,128,128]{1,2,0:T(8,128)(2,1)S(1)} %copy.182, bf16[8,128,128]{1,2,0:T(8,128)(2,1)S(1)} %copy.183, pred[8]{0:T(512)(128)(4,1)S(1)} %iota_compare_fusion.11, bf16[8,4096,128]{2,1,0:T(8,128)(2,1)} %all-to-all-done), kind=kOutput, calls=%fused_computation.63 | convolution fusion | flops 1073872896 | bytes 25690120 | tf_op jit(solution)/shard_map/rbj,bjn->rbn/dot_general | solution.py:105
  751.1 14.0 %fusion.13 = bf16[4096,8,128]{0,2,1:T(8,128)(2,1)} fusion(f32[8,128,4096]{2,1,0:T(8,128)} %fusion.42, bf16[8,4096,128]{2,1,0:T(8,128)(2,1)} %gather_fusion.13, bf16[8,128,128]{1,2,0:T(8,128)(2,1)S(1)} %copy.183, bf16[8,128,128]{1,2,0:T(8,128)(2,1)S(1)} %copy.182, pred[8]{0:T(512)(128)(4,1)S(1)} %iota_compare_fusion.11), kind=kOutput, calls=%fused_computation.30 | convolution fusion | flops 1082261504 | bytes 34078728 | tf_op jit(solution)/shard_map/rbj,bjn->rbn/dot_general | solution.py:108
  765.1 189.9 %all_to_all.32 = bf16[4096,8,128]{0,2,1:T(8,128)(2,1)} all-to-all(bf16[4096,8,128]{0,2,1:T(8,128)(2,1)} %fusion.13), channel_id=1, replica_groups=mesh['orb'=8,'bas'=4] {'orb'}, dimensions={1} | all-to-all | bytes 16777216 | tf_op jit(solution)/shard_map/all_to_all | solution.py:112
  955.0 11.9 %copy.169 = bf16[8,4096,128]{2,1,0:T(8,128)(2,1)} copy(bf16[8,4096,128]{1,2,0:T(8,128)(2,1)} %bitcast.175) | data formatting | bytes 16777216 | tf_op jit(solution)/shard_map/all_to_all | solution.py:112
  (106 shorter events, 16.2 us)
Async XLA Ops:
  6.5 6.5 copy-start.1
  6.5 7.0 copy-start.2
  6.5 190.5 %all-to-all-start = ((bf16[8,4096,128]{2,1,0:T(8,128)(2,1)}), bf16[8,4096,128]{2,1,0:T(8,128)(2,1)}, u32[]{:S(2)}, u32[]{:S(2)}) async-start(bf16[8,4096,128]{2,1,0:T(8,128)(2,1)} %bitcast.178), calls=%async_computation | async-start | bytes 16777216 | tf_op jit(solution)/shard_map/all_to_all | solution.py:76
  13.0 546.4 %all-reduce.3.cloned.1.call-start = ((), (), s32[]{:S(2)}) async-start(), calls=%async_computation.3 | async-start | bytes 9437184
  445.8 5.6 copy-start
  449.2 4.8 copy-start.4
  451.4 110.7 %copy-start.3 = (s32[1,8]{1,0:T(1,128)S(1)}, s32[1,8]{1,0:T(1,128)}, u32[]{:S(2)}) copy-start(s32[1,8]{1,0:T(1,128)} %param.7) | copy-start | bytes 100
  454.0 145.7 %all-gather.3.cloned.1.call-start = ((), (), s32[]{:S(2)}) async-start(), calls=%async_computation.2 | async-start | bytes 2949120 | tf_op jit(solution)/shard_map/all_gather | solution.py:92
Sparse Core Ops, SparseCore 0:
  454.1 105.2 all-reduce.2
  562.1 37.5 all-gather.2
